TPU v7x, 32 devices: a whole 2x2x4 slice. The times are simulated.
32 devices in a mesh: dp: 8 (over y, x, core), tensor: 4 (over z).
Axes of the slice: x: 2, y: 2, z: 4, core: 2. Of those that a mesh axis runs over, the one named last changes fastest.
Arguments:
- token_ids: int32 [4096], P('dp'), may hold values from 0 to 511
- table: bfloat16 [512, 2560], replicated, may hold values from -27 to 27
- weights: bfloat16 [2560, 10240], P(None, 'tensor'), may hold values from -6 to 6
- targets: bfloat16 [4096, 10240], P('dp', 'tensor'), may hold values from -5.5 to 5.5
- momentum: float32 [2560, 10240], P('dp', 'tensor'), may hold values from -6 to 6
Outputs:
- new_weights: bfloat16 [2560, 10240], P(None, 'tensor')
- new_momentum: float32 [2560, 10240], P('dp', 'tensor')
All inputs are finite; a program needn't handle non-finite values.
Results may differ from a plain program's by a relative error of at most 0.0052.
Values may be sent and summed in bfloat16 or wider, within the bound.
A program may use at most 128 MiB of HBM per device.

v0:
```python
import jax
import jax.numpy as jnp
from jax import lax
from jax.sharding import PartitionSpec as P

epsilon = 1e-06
momentum_decay = 0.9
learning_rate = 0.25


def from_partner(value, axis, stride):
    mask = 2**stride
    pairs = [(source, source ^ mask) for source in range(lax.axis_size(axis))]
    return lax.ppermute(value, axis, pairs)


def gelu_tanh(values):
    return jax.nn.gelu(values, approximate=True)


def body(token_ids, table, weights, targets, momentum):
    rows_in = jnp.take(table, token_ids, axis=0)
    preact = jnp.dot(rows_in, weights, preferred_element_type=jnp.float32)
    activated, pullback = jax.vjp(gelu_tanh, preact)
    grad_pre = pullback(activated - targets.astype(jnp.float32))[0].astype(jnp.bfloat16)
    current = lax.dot_general(
        rows_in, grad_pre, (((0,), (0,)), ((), ())), preferred_element_type=jnp.float32
    ).astype(jnp.bfloat16)
    replicas = lax.axis_size("dp")
    tree_depth = replicas.bit_length() - 1
    replica_index = lax.axis_index("dp")
    for tree_level in range(tree_depth):
        pair_bit = tree_depth - 1 - tree_level
        upper_side = replica_index >> pair_bit & 1 == 1
        half_rows = current.shape[0] // 2
        lower_part = current[:half_rows]
        upper_part = current[half_rows:]
        kept_part = jnp.where(upper_side, upper_part, lower_part)
        sent_part = jnp.where(upper_side, lower_part, upper_part)
        received = from_partner(sent_part, "dp", pair_bit)
        own_half = kept_part.astype(jnp.float32)
        peer_half = received.astype(jnp.float32)
        first_vec = jnp.where(upper_side, peer_half, own_half)
        second_vec = jnp.where(upper_side, own_half, peer_half)
        partials = jnp.stack(
            [
                jnp.sum(first_vec * second_vec),
                jnp.sum(first_vec * first_vec),
                jnp.sum(second_vec * second_vec),
            ]
        )
        partials = lax.psum(partials, "tensor")
        for sub_level in range(tree_level + 1):
            partials = partials + from_partner(partials, "dp", tree_depth - 1 - sub_level)
        cross_dot = partials[0]
        first_sq = partials[1]
        second_sq = partials[2]
        combined = (1.0 - cross_dot / (2.0 * (first_sq + epsilon))) * first_vec + (
            1.0 - cross_dot / (2.0 * (second_sq + epsilon))
        ) * second_vec
        if tree_level + 1 < tree_depth:
            current = combined.astype(jnp.bfloat16)
        else:
            current = combined
    new_momentum = momentum_decay * momentum + current
    owned_rows = momentum.shape[0]
    own_weights = lax.dynamic_slice_in_dim(weights, replica_index * owned_rows, owned_rows, 0)
    new_piece = (own_weights.astype(jnp.float32) - learning_rate * new_momentum).astype(
        jnp.bfloat16
    )
    new_weights = lax.all_gather(new_piece, "dp", axis=0, tiled=True)
    return (new_weights, new_momentum)


def solution(mesh):
    placed = (P("dp"), P(), P(None, "tensor"), P("dp", "tensor"), P("dp", "tensor"))
    return jax.shard_map(
        body,
        mesh=mesh,
        in_specs=placed,
        out_specs=(P(None, "tensor"), P("dp", "tensor")),
        check_vma=False,
    )
```

profile of v0, /device:TPU:0, one launch (start us, length us, event | category | flops | bytes accessed | tf_op | source)
XLA Modules:
  0.0 469.8 jit_solution(6130710154469249845)
XLA Ops:
  8.9 3.5 gather_fusion
  12.4 11.0 %fusion.14 = f32[512,2560]{1,0:T(8,128)S(1)} fusion(bf16[2560,2560]{1,0:T(8,128)(2,1)} %param.7, bf16[512,2560]{1,0:T(8,128)(2,1)} %gather_fusion, pred[512]{0:T(512)(128)(4,1)S(1)} %compare_and_fusion), kind=kOutput, calls=%fused_computation.43 | convolution fusion | flops 6712197120 | bytes 20972032 | tf_op jit(solution)/shard_map/dot_general | solution.py:23
  23.4 11.2 %convolution_convert_fusion = bf16[2560,2560]{1,0:T(8,128)(2,1)} fusion(f32[512,2560]{1,0:T(8,128)S(1)} %fusion.14, bf16[512,2560]{1,0:T(8,128)(2,1)S(1)} %copy-done.4, bf16[512,2560]{1,0:T(8,128)(2,1)S(1)} %copy-done.3, pred[512]{0:T(512)(128)(4,1)S(1)} %compare_and_fusion), kind=kOutput, calls=%fused_computation.1 | convolution fusion | flops 6748897280 | bytes 23593472 | tf_op jit(solution)/shard_map/dot_general | solution.py:26
  34.6 8.1 %broadcast_select_fusion.1 = bf16[1280,2560]{1,0:T(8,128)(2,1)} fusion(pred[]{:T(512)S(6)} %eq.11, bf16[2560,2560]{1,0:T(8,128)(2,1)} %convolution_convert_fusion), kind=kLoop, calls=%fused_computation.17 | loop fusion | flops 3276800 | bytes 19660800 | tf_op jit(solution)/shard_map/jit(_where)/select_n | solution.py:39
  42.7 3.0 collective-permute-start
  45.7 141.4 %collective-permute-done = bf16[1280,2560]{1,0:T(8,128)(2,1)} collective-permute-done((bf16[1280,2560]{1,0:T(8,128)(2,1)}, bf16[1280,2560]{1,0:T(8,128)(2,1)}, u32[]{:S(2)}, u32[]{:S(2)}) %collective-permute-start) | collective-permute-done | bytes 6553632 | tf_op jit(solution)/shard_map/ppermute | solution.py:14
  187.1 12.0 %multiply_reduce_fusion.2 = (f32[]{:T(128)}, f32[]{:T(128)}, f32[]{:T(128)}, bf16[1280,2560]{1,0:T(8,128)(2,1)}) fusion(bf16[1280,2560]{1,0:T(8,128)(2,1)} %collective-permute-done, pred[]{:T(512)S(6)} %eq.11, bf16[2560,2560]{1,0:T(8,128)(2,1)} %convolution_convert_fusion), kind=kLoop, calls=%fused_computation.7 | loop fusion | flops 36044800 | bytes 26214412 | tf_op jit(solution)/shard_map/reduce_sum | solution.py:47
  201.1 12.3 %psum.21 = f32[3]{0:T(128)S(1)} all-reduce(f32[3]{0:T(128)S(1)} %pad_maximum_fusion), channel_id=1, replica_groups=mesh['dp'=8,'tensor'=4] {'tensor'}, use_global_device_ids=true, to_apply=%region_3.4 | all-reduce | flops 3 | bytes 24 | tf_op jit(solution)/shard_map/psum | solution.py:52
  215.0 2.0 collective-permute-done.1
  220.1 10.8 %add_convert_fusion = bf16[1280,2560]{1,0:T(8,128)(2,1)} fusion(bf16[1280,2560]{1,0:T(8,128)(2,1)} %get-tuple-element.15, bf16[1280,2560]{1,0:T(8,128)(2,1)} %collective-permute-done, f32[]{:T(128)} %bitcast.4, f32[]{:T(128)} %bitcast.3, pred[]{:T(512)S(6)} %eq.11), kind=kLoop, calls=%fused_computation.4 | loop fusion | flops 26214400 | bytes 19660808 | tf_op jit(solution)/shard_map/convert_element_type | solution.py:62
  231.0 5.0 %broadcast_select_fusion.3 = bf16[640,2560]{1,0:T(8,128)(2,1)} fusion(pred[]{:T(512)S(6)} %eq.10, bf16[1280,2560]{1,0:T(8,128)(2,1)} %add_convert_fusion), kind=kLoop, calls=%fused_computation.33 | loop fusion | flops 1638400 | bytes 9830401 | tf_op jit(solution)/shard_map/jit(_where)/select_n | solution.py:39
  237.4 67.7 %collective-permute-done.2 = bf16[640,2560]{1,0:T(8,128)(2,1)} collective-permute-done((bf16[640,2560]{1,0:T(8,128)(2,1)}, bf16[640,2560]{1,0:T(8,128)(2,1)}, u32[]{:S(2)}, u32[]{:S(2)}) %collective-permute-start.2) | collective-permute-done | bytes 3276832 | tf_op jit(solution)/shard_map/ppermute | solution.py:14
  305.1 7.0 %multiply_reduce_fusion.5 = (f32[]{:T(128)}, f32[]{:T(128)}, f32[]{:T(128)}, bf16[640,2560]{1,0:T(8,128)(2,1)}) fusion(bf16[640,2560]{1,0:T(8,128)(2,1)} %collective-permute-done.2, pred[]{:T(512)S(6)} %eq.10, bf16[1280,2560]{1,0:T(8,128)(2,1)} %add_convert_fusion), kind=kLoop, calls=%fused_computation.15 | loop fusion | flops 18022396 | bytes 13107213 | tf_op jit(solution)/shard_map/reduce_sum | solution.py:47
  314.0 8.3 %psum.22 = f32[3]{0:T(128)S(1)} all-reduce(f32[3]{0:T(128)S(1)} %pad_maximum_fusion.1), channel_id=1, replica_groups=mesh['dp'=8,'tensor'=4] {'tensor'}, use_global_device_ids=true, to_apply=%region_7.8 | all-reduce | flops 3 | bytes 24 | tf_op jit(solution)/shard_map/psum | solution.py:52
  327.5 2.0 collective-permute-done.4
  332.5 4.5 add_convert_fusion.1
  340.1 3.7 collective-permute-done.5
  343.9 5.1 %multiply_reduce_fusion.8 = (f32[]{:T(128)}, f32[]{:T(128)}, f32[]{:T(128)}, bf16[320,2560]{1,0:T(8,128)(2,1)}) fusion(bf16[320,2560]{1,0:T(8,128)(2,1)S(1)} %collective-permute-done.5, pred[]{:T(512)S(6)} %eq.9, bf16[640,2560]{1,0:T(8,128)(2,1)} %copy-done.2), kind=kLoop, calls=%fused_computation.31 | loop fusion | flops 9011197 | bytes 6553613 | tf_op jit(solution)/shard_map/reduce_sum | solution.py:47
  350.9 10.3 %psum.23 = f32[3]{0:T(128)S(1)} all-reduce(f32[3]{0:T(128)S(1)} %pad_maximum_fusion.2), channel_id=1, replica_groups=mesh['dp'=8,'tensor'=4] {'tensor'}, use_global_device_ids=true, to_apply=%region_11.12 | all-reduce | flops 3 | bytes 24 | tf_op jit(solution)/shard_map/psum | solution.py:52
  362.8 2.0 collective-permute-done.6
  366.3 2.0 collective-permute-done.7
  372.8 6.5 %subtract_convert_fusion = (bf16[320,2560]{1,0:T(8,128)(2,1)}, f32[320,2560]{1,0:T(8,128)}) fusion(bf16[2560,2560]{1,0:T(8,128)(2,1)} %param.7, s32[]{:T(128)S(6)} %select_n.78, f32[]{:T(128)} %bitcast.14, bf16[320,2560]{1,0:T(8,128)(2,1)} %get-tuple-element.13, bf16[320,2560]{1,0:T(8,128)(2,1)S(1)} %collective-permute-done.5, pred[]{:T(512)S(6)} %eq.9, ...), kind=kLoop, calls=%fused_computation.27 | loop fusion | flops 10649600 | bytes 13107213 | tf_op jit(solution)/shard_map/convert_element_type | solution.py:68
  379.3 72.7 %all-gather.2.cloned.1.call-done = bf16[2560,2560]{1,0:T(8,128)(2,1)} async-done(((bf16[320,2560]{1,0:T(8,128)(2,1)}), bf16[2560,2560]{1,0:T(8,128)(2,1)}) %all-gather.2.cloned.1.call-update) | async-done | bytes 13107216 | tf_op jit(solution)/shard_map/all_gather | solution.py:71
  452.0 11.0 %copy.8 = bf16[2560,2560]{1,0:T(8,128)(2,1)} copy(bf16[2560,2560]{1,0:T(8,128)(2,1)} %all-gather.2.cloned.1.call-done) | data formatting | bytes 26214400
  (38 shorter events, 24.8 us)
Async XLA Ops:
  7.2 1.8 copy-start
  7.2 444.8 %all-gather.2.cloned.1.call-start = ((), (), s32[]{:S(2)}) async-start(), calls=%async_computation | async-start | bytes 14745600 | tf_op jit(solution)/shard_map/all_gather | solution.py:71
  12.4 11.0 %copy-start.3 = (bf16[512,2560]{1,0:T(8,128)(2,1)S(1)}, bf16[512,2560]{1,0:T(8,128)(2,1)}, u32[]{:S(2)}) copy-start(bf16[512,2560]{1,0:T(8,128)(2,1)} %gather_fusion) | copy-start | bytes 7864324
  12.4 11.0 %copy-start.4 = (bf16[512,2560]{1,0:T(8,128)(2,1)S(1)}, bf16[512,2560]{1,0:T(8,128)(2,1)}, u32[]{:S(2)}) copy-start(bf16[512,2560]{1,0:T(8,128)(2,1)} %param.8) | copy-start | bytes 7864324
  42.7 144.4 %collective-permute-start = (bf16[1280,2560]{1,0:T(8,128)(2,1)}, bf16[1280,2560]{1,0:T(8,128)(2,1)}, u32[]{:S(2)}, u32[]{:S(2)}) collective-permute-start(bf16[1280,2560]{1,0:T(8,128)(2,1)} %broadcast_select_fusion.1), channel_id=1, source_target_pairs={{0,16},{4,20},{8,24},{12,28},{16,0},{20,4},{24,8},{28,12},{1,17},{... | collective-permute-start | bytes 19660808 | tf_op jit(solution)/shard_map/ppermute | solution.py:14
  213.4 3.6 collective-permute-start.1
  235.9 69.2 %collective-permute-start.2 = (bf16[640,2560]{1,0:T(8,128)(2,1)}, bf16[640,2560]{1,0:T(8,128)(2,1)}, u32[]{:S(2)}, u32[]{:S(2)}) collective-permute-start(bf16[640,2560]{1,0:T(8,128)(2,1)} %broadcast_select_fusion.3), channel_id=1, source_target_pairs={{0,8},{4,12},{8,0},{12,4},{16,24},{20,28},{24,16},{28,20},{1,9},{5... | collective-permute-start | bytes 9830408 | tf_op jit(solution)/shard_map/ppermute | solution.py:14
  322.4 3.6 collective-permute-start.3
  326.0 3.5 collective-permute-start.4
  337.1 1.7 copy-start.2
  340.1 3.7 collective-permute-start.5
  361.2 3.6 collective-permute-start.6
  364.8 3.5 collective-permute-start.7
  368.4 1.1 collective-permute-start.8
  452.0 11.0 %copy-start.1 = (bf16[512,2560]{1,0:T(8,128)(2,1)S(1)}, bf16[512,2560]{1,0:T(8,128)(2,1)}, u32[]{:S(2)}) copy-start(bf16[512,2560]{1,0:T(8,128)(2,1)} %param.6) | copy-start | bytes 7864324
Sparse Core Ops, SparseCore 0:
  379.4 72.5 all-gather.1
where the time goes:
time: 470 us
  waiting for transfers between devices  297 us (63%)
  other arithmetic  67.7 us (14%)
  blocking collectives  31 us (7%)
  matrix products  22.2 us (5%)
  between operations  21.7 us (5%)
  local copies, waits for them, and re-layouts  18.2 us (4%)
  starting transfers between devices  12.2 us (3%)
    ppermute x9, waiting for transfers between devices, from_partner(): return lax.ppermute(value, axis, pairs)  224 us
    all_gather x1, waiting for transfers between devices, body(): new_weights = lax.all_gather(new_piece, 'dp', axis=0, tiled=True)  72.7 us
    psum x3, blocking collectives, body(): partials = lax.psum(partials, 'tensor')  31 us
    reduce_sum x3, other arithmetic, body(): jnp.sum(first_vec * second_vec)  24.1 us
    convert_element_type x2, other arithmetic, body(): current = combined.astype(jnp.bfloat16)  15.4 us
    select_n x3, other arithmetic, body(): sent_part = jnp.where(upper_side, lower_part, upper_part)  14.4 us
    unnamed x11, local copies, waits for them, and re-layouts  12.9 us
    ppermute x9, starting transfers between devices, from_partner(): return lax.ppermute(value, axis, pairs)  12.2 us
  transfers between devices with their start and end apart: 10, of which 10 were waited for; matrix products, arithmetic and copies ran while one was open for 0% of the time, Pallas kernels for 0%

commit v1 on v0

v1 whole, which is shorter than its diff:
```python
import jax
import jax.numpy as jnp
from jax import lax
from jax.sharding import PartitionSpec as P

epsilon = 1e-06
momentum_decay = 0.9
learning_rate = 0.25


def gelu_tanh(values):
    return jax.nn.gelu(values, approximate=True)


def row_grads(token_ids, table, weights, targets):
    row = lax.broadcasted_iota(jnp.int32, (table.shape[0], token_ids.shape[0]), 0)
    hot = row == token_ids[None, :]
    count = jnp.sum(hot.astype(jnp.float32), axis=1, keepdims=True)
    target_sum = jnp.dot(hot.astype(jnp.bfloat16), targets, preferred_element_type=jnp.float32)
    preact = jnp.dot(table, weights, preferred_element_type=jnp.float32)
    activated, pullback = jax.vjp(gelu_tanh, preact)
    return pullback(count * activated - target_sum)[0].astype(jnp.bfloat16)


def split_kernel(table):
    kern = lax.dot_general(
        table, table, (((1,), (1,)), ((), ())), preferred_element_type=jnp.float32
    )
    high = kern.astype(jnp.bfloat16)
    return high, (kern - high.astype(jnp.float32)).astype(jnp.bfloat16)


def tree_coefficients(gram):
    replicas = gram.shape[0]
    vecs = jnp.eye(replicas, dtype=jnp.float32)
    while vecs.shape[0] > 1:
        half = vecs.shape[0] // 2
        low, high = vecs[:half], vecs[half:]
        low_g = jnp.sum(low[:, :, None] * gram[None], axis=1)
        high_g = jnp.sum(high[:, :, None] * gram[None], axis=1)
        cross = jnp.sum(low_g * high, axis=1, keepdims=True)
        low_sq = jnp.maximum(jnp.sum(low_g * low, axis=1, keepdims=True), 0.0)
        high_sq = jnp.maximum(jnp.sum(high_g * high, axis=1, keepdims=True), 0.0)
        vecs = (1.0 - cross / (2.0 * (low_sq + epsilon))) * low + (
            1.0 - cross / (2.0 * (high_sq + epsilon))
        ) * high
    return vecs[0]


def body(token_ids, table, weights, targets, momentum):
    replicas = lax.axis_size("dp")
    me = lax.axis_index("dp")
    all_momentum = lax.all_gather(momentum.astype(jnp.bfloat16), "dp", axis=0, tiled=True)
    grads = row_grads(token_ids, table, weights, targets)
    rows, cols = grads.shape
    own = lax.all_to_all(grads, "dp", split_axis=1, concat_axis=0, tiled=True)
    own = own.reshape(replicas, rows, cols // replicas)
    high, low = split_kernel(table)
    gram = []
    for other in range(replicas):
        mapped = jnp.dot(high, own[other], preferred_element_type=jnp.float32) + jnp.dot(
            low, own[other], preferred_element_type=jnp.float32
        )
        gram.append(jnp.sum(own.astype(jnp.float32) * mapped[None], axis=(1, 2)))
    gram = lax.psum(jnp.stack(gram), ("dp", "tensor"))
    coefs = tree_coefficients(gram)
    mixed = jnp.sum(own.astype(jnp.float32) * coefs[:, None, None], axis=0).astype(jnp.bfloat16)
    mixed = lax.all_gather(mixed, "dp", axis=1, tiled=True)
    adasum = lax.dot_general(
        table, mixed, (((0,), (0,)), ((), ())), preferred_element_type=jnp.float32
    )
    owned = momentum.shape[0]
    own_table = lax.dynamic_slice_in_dim(table, me * owned, owned, 1)
    own_adasum = lax.dot_general(
        own_table, mixed, (((0,), (0,)), ((), ())), preferred_element_type=jnp.float32
    )
    new_momentum = momentum_decay * momentum + own_adasum
    new_weights = (
        weights.astype(jnp.float32)
        - learning_rate * (momentum_decay * all_momentum.astype(jnp.float32) + adasum)
    ).astype(jnp.bfloat16)
    return (new_weights, new_momentum)


def solution(mesh):
    placed = (P("dp"), P(), P(None, "tensor"), P("dp", "tensor"), P("dp", "tensor"))
    return jax.shard_map(
        body,
        mesh=mesh,
        in_specs=placed,
        out_specs=(P(None, "tensor"), P("dp", "tensor")),
        check_vma=False,
    )
```

time: 470 us -> 311 us (0.66)
  waiting for transfers between devices: 297 us -> 110 us
  other arithmetic: 67.7 us -> 15.1 us
  matrix products: 22.2 us -> 63.1 us
  local copies, waits for them, and re-layouts: 18.2 us -> 58.2 us
  blocking collectives: 31 us -> 40.3 us
  starting transfers between devices: 12.2 us -> 5.25 us
  between operations: 21.7 us -> 16.8 us
    ppermute x9 -> x0, waiting for transfers between devices: 224 us -> none  [from_partner(): return lax.ppermute(value, axis, pairs)]
    dot_general x2 -> x21, matrix products: 22.2 us -> 63.1 us  [the longest x1 17.2 us: body(): lax.dot_general(table, mixed, (((0,), (0,)), ((), ())), preferred_element...]
    all_to_all x0 -> x1, waiting for transfers between devices: none -> 30 us  [body(): own = lax.all_to_all(grads, 'dp', split_axis=1, concat_axis=0, tiled=True)]
    unnamed x11 -> x10, local copies, waits for them, and re-layouts: 12.9 us -> 36.2 us
    convert_element_type x3 -> x2, other arithmetic: 21.9 us -> 3.26 us  [the longest x1 3.26 us: body(): momentum.astype(jnp.bfloat16)]
    all_gather x0 -> x1, local copies, waits for them, and re-layouts: none -> 17.6 us  [body(): lax.all_gather(momentum.astype(jnp.bfloat16), 'dp', axis=0, tiled=True)]
    select_n x4 -> x0, other arithmetic: 15.1 us -> none  [the longest x3 14.4 us: body(): sent_part = jnp.where(upper_side, lower_part, upper_part)]
    reduce_sum x3 -> x9, other arithmetic: 24.1 us -> 11.7 us  [the longest x1 6.3 us: body(): gram.append(jnp.sum(own.astype(jnp.float32) * mapped[None], axis=(1, 2)))]
  transfers between devices with their start and end apart: 10 -> 3, of which waited for: 10 -> 3; matrix products, arithmetic and copies ran while one was open for 0% -> 10% of each run, Pallas kernels for 0% -> 0%
where the time goes in v1:
time: 311 us; the launch traced here: 309 us
  waiting for transfers between devices  110 us (35%)
  matrix products  63.1 us (20%)
  local copies, waits for them, and re-layouts  58.2 us (19%)
  blocking collectives  40.3 us (13%)
  between operations  16.8 us (5%)
  other arithmetic  15.1 us (5%)
  starting transfers between devices  5.25 us (2%)
    all_gather x1, waiting for transfers between devices, body(): lax.all_gather(momentum.astype(jnp.bfloat16), 'dp', axis=0, tiled=True)  71 us
    psum x1, blocking collectives, body(): gram = lax.psum(jnp.stack(gram), ('dp', 'tensor'))  40.3 us
    unnamed x10, local copies, waits for them, and re-layouts  36.2 us
    all_to_all x1, waiting for transfers between devices, body(): own = lax.all_to_all(grads, 'dp', split_axis=1, concat_axis=0, tiled=True)  30 us
    all_gather x1, local copies, waits for them, and re-layouts, body(): lax.all_gather(momentum.astype(jnp.bfloat16), 'dp', axis=0, tiled=True)  17.6 us
    dot_general x1, matrix products, body(): lax.dot_general(table, mixed, (((0,), (0,)), ((), ())), preferred_element...  17.2 us
    dot_general x8, matrix products, body(): jnp.dot(low, own[other], preferred_element_type=jnp.float32)  10.7 us
    dot_general x8, matrix products, body(): jnp.dot(high, own[other], preferred_element_type=jnp.float32)  10.7 us
  transfers between devices with their start and end apart: 3, of which 3 were waited for; matrix products, arithmetic and copies ran while one was open for 10% of the time, Pallas kernels for 0%

profile of v1, /device:TPU:0, one launch (start us, length us, event | category | flops | bytes accessed | tf_op | source)
XLA Modules:
  0.0 308.7 jit_solution(7085606771398435866)
XLA Ops:
  8.9 10.1 %fusion.40 = f32[512,2560]{1,0:T(8,128)S(1)} fusion(bf16[512,2560]{1,0:T(8,128)(2,1)S(1)} %copy-done, bf16[2560,2560]{1,0:T(8,128)(2,1)} %param.7), kind=kOutput, calls=%fused_computation.97 | convolution fusion | flops 6710886400 | bytes 20971520 | tf_op jit(solution)/shard_map/dot_general | solution.py:20
  19.1 6.2 %fusion.9 = bf16[512,2560]{1,0:T(8,128)(2,1)} fusion(f32[512,2560]{1,0:T(8,128)S(1)} %fusion.40, bf16[512,2560]{1,0:T(8,128)(2,1)S(1)} %copy-done.3, f32[512]{0:T(512)S(1)} %convert_reduce_fusion, s32[512]{0:T(512)S(1)} %copy-done.2), kind=kOutput, calls=%fused_computation.21 | convolution fusion | flops 1372585984 | bytes 10489856 | tf_op jit(solution)/shard_map/dot_general | solution.py:19
  25.2 4.4 %copy.28 = bf16[512,2560]{0,1:T(8,128)(2,1)} copy(bf16[512,2560]{1,0:T(8,128)(2,1)} %fusion.9) | data formatting | bytes 5242880 | tf_op jit(solution)/shard_map/convert_element_type | solution.py:22
  29.6 5.2 %all-to-all-start = ((bf16[512,8,320]{0,2,1:T(8,128)(2,1)}), bf16[512,8,320]{0,2,1:T(8,128)(2,1)}, u32[]{:S(2)}, u32[]{:S(2)}) async-start(bf16[512,8,320]{0,2,1:T(8,128)(2,1)} %bitcast.100), calls=%async_computation | async-start | bytes 5242880 | tf_op jit(solution)/shard_map/all_to_all | solution.py:56
  34.9 2.3 subtract_convert_fusion
  37.2 30.0 %all-to-all-done = bf16[512,8,320]{0,2,1:T(8,128)(2,1)} async-done(((bf16[512,8,320]{0,2,1:T(8,128)(2,1)}), bf16[512,8,320]{0,2,1:T(8,128)(2,1)}, u32[]{:S(2)}, u32[]{:S(2)}) %all-to-all-start) | async-done | bytes 2621472 | tf_op jit(solution)/shard_map/all_to_all | solution.py:56
  68.5 1.4 fusion.27
  80.6 1.3 convolution_add_fusion.3
  82.0 1.3 convolution_add_fusion.4
  83.3 1.3 convolution_add_fusion.5
  84.7 1.3 convolution_add_fusion.6
  86.0 1.3 convolution_add_fusion.7
  87.4 1.3 convolution_add_fusion.8
  88.7 6.3 %fusion.17 = (f32[8]{0:T(128)S(1)}, f32[8]{0:T(128)S(1)}, f32[8]{0:T(128)S(1)}, f32[8]{0:T(128)S(1)}, f32[8]{0:T(128)S(1)}, /*index=5*/f32[8]{0:T(128)S(1)}, f32[8]{0:T(128)S(1)}, f32[8]{0:T(128)S(1)}) fusion(f32[512,320]{0,1:T(8,128)S(1)} %convolution_add_fusion.1, bf16[512,8,320]{0,2,1:T(8,128)(2,1)} %all-to-all-done, ...), kind=kLoop, calls=%fused_computation.29 | loop fusion | flops 22282176 | bytes 7864576 | tf_op jit(solution)/shard_map/reduce_sum | solution.py:64
  95.1 40.3 %psum.7 = f32[8,8]{1,0:T(8,128)S(1)} all-reduce(f32[8,8]{1,0:T(8,128)S(1)} %stack.35), channel_id=1, replica_groups=mesh['dp'=8,'tensor'=4] {'dp','tensor'}, use_global_device_ids=true, to_apply=%region_9.0 | all-reduce | flops 64 | bytes 512 | tf_op jit(solution)/shard_map/psum | solution.py:65
  139.3 3.1 %fusion.18 = bf16[512,320]{0,1:T(8,128)(2,1)} fusion(f32[8]{0:T(128)S(1)} %add_bitcast_fusion, bf16[512,8,320]{0,2,1:T(8,128)(2,1)} %all-to-all-done), kind=kLoop, calls=%fused_computation.30 | loop fusion | flops 3768320 | bytes 2949152 | tf_op jit(solution)/shard_map/reduce_sum | solution.py:67
  142.6 3.3 %convert_element_type.58 = bf16[320,2560]{1,0:T(8,128)(2,1)} convert(f32[320,2560]{1,0:T(8,128)} %param.9) | non-fusion elementwise | flops 819200 | bytes 4915200 | tf_op jit(solution)/shard_map/convert_element_type | solution.py:53
  145.8 17.9 %copy.26 = bf16[2560,2560]{0,1:T(8,128)(2,1)} copy(bf16[2560,2560]{1,0:T(8,128)(2,1)} %param.7) | data formatting | bytes 26214400 | tf_op args[2]
  163.7 9.0 %all-gather.5.cloned.1.call-done = bf16[512,2560]{0,1:T(8,128)(2,1)} async-done(((bf16[512,320]{0,1:T(8,128)(2,1)}), bf16[512,2560]{0,1:T(8,128)(2,1)}) %all-gather.5.cloned.1.call-update) | async-done | bytes 2621456 | tf_op jit(solution)/shard_map/all_gather | solution.py:68
  172.7 5.9 %convolution_add_fusion = f32[320,2560]{1,0:T(8,128)} fusion(bf16[512,2560]{0,1:T(8,128)(2,1)} %all-gather.5.cloned.1.call-done, f32[320,2560]{1,0:T(8,128)} %param.9, bf16[512,2560]{1,0:T(8,128)(2,1)S(1)} %copy-done, s32[]{:T(128)S(6)} %select_n.3), kind=kOutput, calls=%fused_computation.31 | convolution fusion | flops 840499200 | bytes 9568260 | tf_op jit(solution)/shard_map/dot_general | solution.py:74
  178.6 71.0 %all-gather.3.cloned.1.call-done = bf16[2560,2560]{1,0:T(8,128)(2,1)} async-done(((bf16[320,2560]{1,0:T(8,128)(2,1)}), bf16[2560,2560]{1,0:T(8,128)(2,1)}) %all-gather.3.cloned.1.call-update) | async-done | bytes 13107216 | tf_op jit(solution)/shard_map/all_gather | solution.py:53
  249.5 17.6 %copy.27 = bf16[2560,2560]{0,1:T(8,128)(2,1)} copy(bf16[2560,2560]{1,0:T(8,128)(2,1)} %all-gather.3.cloned.1.call-done) | data formatting | bytes 26214400 | tf_op jit(solution)/shard_map/all_gather | solution.py:53
  267.1 17.2 %fusion.2 = bf16[2560,2560]{0,1:T(8,128)(2,1)} fusion(bf16[2560,2560]{0,1:T(8,128)(2,1)} %copy.27, bf16[2560,2560]{0,1:T(8,128)(2,1)} %copy.26, bf16[512,2560]{0,1:T(8,128)(2,1)} %all-gather.5.cloned.1.call-done, bf16[512,2560]{1,0:T(8,128)(2,1)S(1)} %copy-done), kind=kOutput, calls=%fused_computation.3 | convolution fusion | flops 6756761600 | bytes 44564480 | tf_op jit(solution)/shard_map/dot_general | solution.py:69
  284.3 17.6 %copy.29 = bf16[2560,2560]{1,0:T(8,128)(2,1)} copy(bf16[2560,2560]{0,1:T(8,128)(2,1)} %fusion.2) | data formatting | bytes 26214400
  (38 shorter events, 15.3 us)
Async XLA Ops:
  7.2 1.8 copy-start
  8.9 10.1 %copy-start.2 = (s32[512]{0:T(512)S(1)}, s32[512]{0:T(512)}, u32[]{:S(2)}) copy-start(s32[512]{0:T(512)} %param.5) | copy-start | bytes 6148
  8.9 10.1 %copy-start.3 = (bf16[512,2560]{1,0:T(8,128)(2,1)S(1)}, bf16[512,2560]{1,0:T(8,128)(2,1)}, u32[]{:S(2)}) copy-start(bf16[512,2560]{1,0:T(8,128)(2,1)} %param.8) | copy-start | bytes 7864324
  29.6 37.5 %all-to-all-start = ((bf16[512,8,320]{0,2,1:T(8,128)(2,1)}), bf16[512,8,320]{0,2,1:T(8,128)(2,1)}, u32[]{:S(2)}, u32[]{:S(2)}) async-start(bf16[512,8,320]{0,2,1:T(8,128)(2,1)} %bitcast.100), calls=%async_computation | async-start | bytes 5242880 | tf_op jit(solution)/shard_map/all_to_all | solution.py:56
  34.8 137.9 %all-gather.5.cloned.1.call-start = ((), (), s32[]{:S(2)}) async-start(), calls=%async_computation.2 | async-start | bytes 2949120 | tf_op jit(solution)/shard_map/all_gather | solution.py:68
  68.5 9.4 %copy-start.1 = (bf16[512,512]{1,0:T(8,128)(2,1)S(1)}, bf16[512,512]{1,0:T(8,128)(2,1)}, u32[]{:S(2)}) copy-start(bf16[512,512]{1,0:T(8,128)(2,1)} %get-tuple-element.33) | copy-start | bytes 1572868
  142.5 107.0 %all-gather.3.cloned.1.call-start = ((), (), s32[]{:S(2)}) async-start(), calls=%async_computation.1 | async-start | bytes 14745600 | tf_op jit(solution)/shard_map/all_gather | solution.py:53
Sparse Core Ops, SparseCore 0:
  142.6 30.0 all-gather.4
  175.2 74.3 all-gather.2

commit v2 on v1

--- a/solution.py
+++ b/solution.py
@@ -1,6 +1,8 @@
 import jax
 import jax.numpy as jnp
 from jax import lax
+from jax.experimental import pallas as pl
+from jax.experimental.pallas import tpu as pltpu
 from jax.sharding import PartitionSpec as P
 
 epsilon = 1e-06
@@ -82,10 +84,448 @@
     return (new_weights, new_momentum)
 
 
+MESH = pl.DeviceIdType.MESH
+
+
+def flip(index, bits):
+    out = 0
+    for place in (4, 2, 1):
+        bit = lax.rem(lax.div(index, place), 2)
+        out = out + place * lax.rem(bit + lax.rem(lax.div(bits, place), 2), 2)
+    return out
+
+
+class Gather:
+    def __init__(self, me, own, out, send, recv, parts):
+        self.me, self.own, self.out, self.send, self.recv = me, own, out, send, recv
+        self.parts, self.piece = parts, own.shape[0]
+        self.rows = self.piece // parts
+
+    def place(self, owner, part):
+        start = pl.multiple_of(owner * self.piece + part * self.rows, 16)
+        return self.out.at[pl.ds(start, self.rows)]
+
+    def moved(self, kind, part):
+        if kind in (0, 1, 3):
+            owner, towards = 0, {0: 2, 1: 4, 3: 1}[kind]
+        elif kind == 2:
+            owner, towards = (2, 4) if part < self.parts // 2 else (4, 2)
+        else:
+            owner, towards = {4: 2, 5: 4, 6: 6}[kind], 1
+        return owner, towards
+
+    def copy(self, kind, part):
+        owner, towards = self.moved(kind, part)
+        here = self.place(flip(self.me, owner), part)
+        source = self.own.at[pl.ds(part * self.rows, self.rows)] if owner == 0 else here
+        return pltpu.make_async_remote_copy(
+            src_ref=source,
+            dst_ref=here,
+            send_sem=self.send.at[kind, part],
+            recv_sem=self.recv.at[kind, part],
+            device_id={"dp": flip(self.me, towards)},
+            device_id_type=MESH,
+        )
+
+    def arrived(self, kind, part):
+        owner, towards = self.moved(kind, part)
+        here = self.place(flip(self.me, owner ^ towards), part)
+        pltpu.make_async_remote_copy(
+            src_ref=here,
+            dst_ref=here,
+            send_sem=self.send.at[kind, part],
+            recv_sem=self.recv.at[kind, part],
+            device_id={"dp": flip(self.me, towards)},
+            device_id_type=MESH,
+        ).wait_recv()
+
+
+def exchange(axis, size, value, sent, slots, send, recv):
+    me = lax.axis_index(axis)
+    sent[...] = value
+    slots[me] = value
+    copies = []
+    for shift in range(1, size):
+        copies.append(
+            pltpu.make_async_remote_copy(
+                src_ref=sent,
+                dst_ref=slots.at[me],
+                send_sem=send.at[shift],
+                recv_sem=recv.at[shift],
+                device_id={axis: lax.rem(me + shift, size)},
+                device_id_type=MESH,
+            )
+        )
+        copies[-1].start()
+    for shift in range(1, size):
+        origin = lax.rem(me + size - shift, size)
+        pltpu.make_async_remote_copy(
+            src_ref=sent,
+            dst_ref=slots.at[origin],
+            send_sem=send.at[shift],
+            recv_sem=recv.at[shift],
+            device_id={axis: origin},
+            device_id_type=MESH,
+        ).wait_recv()
+    total = slots[0]
+    for index in range(1, size):
+        total = total + slots[index]
+    return total, copies
+
+
+def tree_columns(gram):
+    rows = lax.broadcasted_iota(jnp.int32, gram.shape, 0)
+    lanes = lax.broadcasted_iota(jnp.int32, (1, gram.shape[1]), 1)
+    vecs = [
+        ((rows == index).astype(jnp.float32), (lanes == index).astype(jnp.float32))
+        for index in range(8)
+    ]
+
+    def inner(left, right):
+        mapped = jnp.sum(left[0] * gram, axis=0, keepdims=True)
+        return jnp.broadcast_to(jnp.sum(mapped * right[1], axis=1, keepdims=True), lanes.shape)
+
+    while len(vecs) > 1:
+        half = len(vecs) // 2
+        merged = []
+        for low, high in zip(vecs[:half], vecs[half:]):
+            cross = inner(low, high)
+            low_sq = jnp.maximum(inner(low, low), 0.0)
+            high_sq = jnp.maximum(inner(high, high), 0.0)
+            first = 1.0 - cross / (2.0 * (low_sq + epsilon))
+            second = 1.0 - cross / (2.0 * (high_sq + epsilon))
+            merged.append(
+                (first * low[0] + second * high[0], first * low[1] + second * high[1])
+            )
+        vecs = merged
+    return vecs[0][0]
+
+
+def mix_kernel(
+    ids, table, weights, targets, momentum, mix_out, mom_out,
+    wbuf, tbuf, gt, gx, kern_high, kern_low, mapped, sums, coef_buf, mix_own,
+    t_sent, t_slots, d_sent, d_slots,
+    w_sem, t_sem, local_sem, mom_send, mom_recv, mix_send, mix_recv,
+    g_send, g_recv, ts_send, ts_recv, ds_send, ds_recv,
+):
+    me = lax.axis_index("dp")
+    mine = lax.axis_index("tensor")
+    chip, core = lax.div(me, 2), lax.rem(me, 2)
+    width = wbuf.shape[2]
+    chunk = gt.shape[1]
+
+    def block(step):
+        return lax.div(flip(2 * chip, 2 * lax.rem(step + 1, 4)), 2)
+
+    def fetch(step, slot):
+        at = pl.ds(pl.multiple_of(block(step) * width, 128), width)
+        return (
+            pltpu.make_async_copy(weights.at[:, at], wbuf.at[slot], w_sem.at[slot]),
+            pltpu.make_async_copy(targets.at[:, at], tbuf.at[slot], t_sem.at[slot]),
+        )
+
+    for load in fetch(0, 0):
+        load.start()
+
+    barrier = pltpu.get_barrier_semaphore()
+    for shift in range(1, 8):
+        pl.semaphore_signal(
+            barrier, inc=1, device_id={"dp": lax.rem(me + shift, 8)}, device_id_type=MESH
+        )
+    for shift in range(1, 4):
+        pl.semaphore_signal(
+            barrier, inc=1, device_id={"tensor": lax.rem(mine + shift, 4)}, device_id_type=MESH
+        )
+    pl.semaphore_wait(barrier, 10)
+
+    mom = Gather(me, momentum, mom_out, mom_send, mom_recv, 4)
+    mix = Gather(me, mix_own, mix_out, mix_send, mix_recv, 2)
+    own_rows = pl.ds(pl.multiple_of(me * mom.piece, 16), mom.piece)
+    keep_mom = pltpu.make_async_copy(momentum, mom_out.at[own_rows], local_sem.at[0])
+    keep_mom.start()
+    for part in (0, 1):
+        mom.copy(0, part).start()
+        mom.copy(1, part + 2).start()
+    for part in range(4):
+        mom.copy(3, part).start()
+
+    row = lax.broadcasted_iota(jnp.int32, (table.shape[0], ids.shape[1]), 0)
+    hot = (row == ids[...]).astype(jnp.float32)
+    count = jnp.sum(hot, axis=1, keepdims=True)
+    hot = hot.astype(jnp.bfloat16)
+
+    def sent_grad(step, other):
+        bits = 2 * lax.rem(step + 1, 4) + other
+        target = flip(me, bits)
+        return pltpu.make_async_remote_copy(
+            src_ref=gt.at[target],
+            dst_ref=gx.at[me],
+            send_sem=g_send.at[bits],
+            recv_sem=g_recv.at[bits],
+            device_id={"dp": target},
+            device_id_type=MESH,
+        )
+
+    def grads(step, carry):
+        slot = lax.rem(step, 2)
+        for load in fetch(step, slot):
+            load.wait()
+
+        @pl.when(step < 3)
+        def _():
+            for load in fetch(step + 1, 1 - slot):
+                load.start()
+
+        x = jnp.dot(table[...], wbuf[slot], preferred_element_type=jnp.float32)
+        target_sum = jnp.dot(hot, tbuf[slot], preferred_element_type=jnp.float32)
+        scale = 0.7978845608028654
+        square = x * x
+        tanh = jnp.tanh(scale * (x + 0.044715 * (square * x)))
+        half = 0.5 * (1.0 + tanh)
+        slope = half + 0.5 * x * (1.0 - tanh * tanh) * (scale * (1.0 + 3 * 0.044715 * square))
+        grad = (slope * (count * (x * half) - target_sum)).T.astype(jnp.bfloat16)
+        dest = block(step)
+        gt[2 * dest] = grad[:chunk]
+        gt[2 * dest + 1] = grad[chunk:]
+
+        @pl.when(step < 3)
+        def _():
+            sent_grad(step, 0).start()
+
+        sent_grad(step, 1).start()
+        return carry
+
+    lax.fori_loop(0, 4, grads, 0)
+    gx[me] = gt[me]
+
+    for part in (0, 1):
+        mom.copy(1, part).start()
+        mom.copy(0, part + 2).start()
+
+    kern = lax.dot_general(
+        table[...], table[...], (((1,), (1,)), ((), ())), preferred_element_type=jnp.float32
+    )
+    high = kern.astype(jnp.bfloat16)
+    kern_high[...] = high
+    kern_low[...] = (kern - high.astype(jnp.float32)).astype(jnp.bfloat16)
+
+    for part in (0, 1):
+        mom.arrived(0, part)
+        mom.copy(2, part).start()
+        mom.copy(4, part).start()
+        mom.arrived(1, part + 2)
+        mom.copy(2, part + 2).start()
+        mom.copy(5, part + 2).start()
+
+    def grams(bits, carry):
+        source = flip(me, bits)
+
+        @pl.when(bits > 0)
+        def _():
+            pltpu.make_async_remote_copy(
+                src_ref=gt.at[source],
+                dst_ref=gx.at[source],
+                send_sem=g_send.at[bits],
+                recv_sem=g_recv.at[bits],
+                device_id={"dp": source},
+                device_id_type=MESH,
+            ).wait_recv()
+
+        mapped[...] = jnp.dot(
+            gx[source], kern_high[...], preferred_element_type=jnp.float32
+        ) + jnp.dot(gx[source], kern_low[...], preferred_element_type=jnp.float32)
+
+        def pair(other, inner_carry):
+            partner = flip(me, other)
+            total = jnp.sum(
+                gx[partner].astype(jnp.float32) * mapped[...], axis=0, keepdims=True
+            )
+            sums[source, pl.ds(partner, 1), :] = total
+            sums[partner, pl.ds(source, 1), :] = total
+            return inner_carry
+
+        lax.fori_loop(0, bits + 1, pair, 0)
+        return carry
+
+    lax.fori_loop(0, 8, grams, 0)
+
+    lanes = lax.broadcasted_iota(jnp.int32, (8, 128), 1)
+    gram = jnp.zeros((8, 128), jnp.float32)
+    for index in range(8):
+        column = jnp.sum(sums[index], axis=1, keepdims=True)
+        gram = gram + jnp.where(lanes == index, column, 0.0)
+    gram, t_copies = exchange("tensor", 4, gram, t_sent, t_slots, ts_send, ts_recv)
+    gram, d_copies = exchange("dp", 8, gram, d_sent, d_slots, ds_send, ds_recv)
+    coef_buf[...] = tree_columns(gram)
+
+    for lane in range(gx.shape[2] // 128):
+        at = pl.ds(lane * 128, 128)
+        total = coef_buf[0:1, :] * gx[0, :, at].astype(jnp.float32)
+        for index in range(1, 8):
+            total = total + coef_buf[index : index + 1, :] * gx[index, :, at].astype(jnp.float32)
+        mix_own[:, at] = total.astype(jnp.bfloat16)
+
+    keep_mix = pltpu.make_async_copy(
+        mix_own,
+        mix_out.at[pl.ds(pl.multiple_of(me * chunk, 16), chunk)],
+        local_sem.at[1],
+    )
+    keep_mix.start()
+    mix.copy(0, 0).start()
+    mix.copy(1, 1).start()
+    mix.copy(0, 1).start()
+    mix.copy(1, 0).start()
+    for part in (0, 1):
+        mix.copy(3, part).start()
+
+    mix.arrived(0, 0)
+    mix.copy(2, 0).start()
+    mix.copy(4, 0).start()
+    mix.arrived(1, 1)
+    mix.copy(2, 1).start()
+    mix.copy(5, 1).start()
+    for part in (0, 1):
+        mom.arrived(1, part)
+        mom.copy(5, part).start()
+        mom.arrived(0, part + 2)
+        mom.copy(4, part + 2).start()
+    for part in range(4):
+        mom.arrived(2, part)
+        mom.copy(6, part).start()
+    mix.arrived(0, 1)
+    mix.copy(4, 1).start()
+    mix.arrived(1, 0)
+    mix.copy(5, 0).start()
+    for part in (0, 1):
+        mix.arrived(2, part)
+        mix.copy(6, part).start()
+
+    for gather in (mom, mix):
+        for part in range(gather.parts):
+            for kind in (3, 4, 5, 6):
+                gather.arrived(kind, part)
+            for kind in range(7):
+                gather.copy(kind, part).wait_send()
+    for step in range(4):
+        if step < 3:
+            sent_grad(step, 0).wait_send()
+        sent_grad(step, 1).wait_send()
+    for copy in t_copies + d_copies:
+        copy.wait_send()
+    keep_mom.wait()
+    keep_mix.wait()
+
+
+def mixed_grads(token_ids, table, weights, targets, momentum):
+    rows, depth = table.shape
+    cols = weights.shape[1]
+    chunk = cols // 8
+    width = 2 * chunk
+    anywhere = pl.BlockSpec(memory_space=pl.ANY)
+    resident = pl.BlockSpec(memory_space=pltpu.VMEM)
+    dma = pltpu.SemaphoreType.DMA
+    bf16, f32 = jnp.bfloat16, jnp.float32
+    return pl.pallas_call(
+        mix_kernel,
+        out_shape=(
+            jax.ShapeDtypeStruct((cols, rows), bf16),
+            jax.ShapeDtypeStruct((8 * momentum.shape[0], cols), bf16),
+        ),
+        in_specs=[resident, resident, anywhere, anywhere, anywhere],
+        out_specs=(anywhere, anywhere),
+        scratch_shapes=[
+            pltpu.VMEM((2, depth, width), bf16),
+            pltpu.VMEM((2, targets.shape[0], width), bf16),
+            pltpu.VMEM((8, chunk, rows), bf16),
+            pltpu.VMEM((8, chunk, rows), bf16),
+            pltpu.VMEM((rows, rows), bf16),
+            pltpu.VMEM((rows, rows), bf16),
+            pltpu.VMEM((chunk, rows), f32),
+            pltpu.VMEM((8, 8, rows), f32),
+            pltpu.VMEM((8, 128), f32),
+            pltpu.VMEM((chunk, rows), bf16),
+            pltpu.VMEM((8, 128), f32),
+            pltpu.VMEM((4, 8, 128), f32),
+            pltpu.VMEM((8, 128), f32),
+            pltpu.VMEM((8, 8, 128), f32),
+            dma((2,)), dma((2,)), dma((2,)),
+            dma((7, 4)), dma((7, 4)), dma((7, 2)), dma((7, 2)),
+            dma((8,)), dma((8,)), dma((4,)), dma((4,)), dma((8,)), dma((8,)),
+        ],
+        compiler_params=pltpu.CompilerParams(
+            collective_id=0, has_side_effects=True, vmem_limit_bytes=56 * 2**20
+        ),
+        cost_estimate=pl.CostEstimate(
+            flops=2 * rows * depth * cols, bytes_accessed=2 * depth * cols, transcendentals=0
+        ),
+    )(token_ids[None, :], table, weights, targets, momentum)
+
+
+def update_kernel(table, own_table, mix, weights, all_momentum, momentum, new_weights, new_momentum):
+    def spread(columns):
+        return lax.dot_general(
+            columns.T, mix[...], (((1,), (1,)), ((), ())), preferred_element_type=jnp.float32
+        )
+
+    @pl.when(pl.program_id(0) == 0)
+    def _():
+        new_momentum[...] = momentum_decay * momentum[...] + spread(own_table[...])
+
+    step = momentum_decay * all_momentum[...].astype(jnp.float32) + spread(table[...])
+    new_weights[...] = (weights[...].astype(jnp.float32) - learning_rate * step).astype(
+        jnp.bfloat16
+    )
+
+
+def updated(table, own_table, mix, weights, all_momentum, momentum):
+    rows, depth = table.shape
+    cols = weights.shape[1]
+    tile = 256
+    owned = momentum.shape[0]
+
+    def whole(shape):
+        return pl.BlockSpec(shape, lambda step: (0, 0))
+
+    def by_rows():
+        return pl.BlockSpec((tile, cols), lambda step: (step, 0))
+
+    return pl.pallas_call(
+        update_kernel,
+        grid=(depth // tile,),
+        out_shape=(
+            jax.ShapeDtypeStruct((depth, cols), jnp.bfloat16),
+            jax.ShapeDtypeStruct((owned, cols), jnp.float32),
+        ),
+        in_specs=[
+            pl.BlockSpec((rows, tile), lambda step: (0, step)),
+            whole((rows, owned)),
+            whole((cols, rows)),
+            by_rows(),
+            by_rows(),
+            whole((owned, cols)),
+        ],
+        out_specs=(by_rows(), whole((owned, cols))),
+        compiler_params=pltpu.CompilerParams(vmem_limit_bytes=56 * 2**20),
+        cost_estimate=pl.CostEstimate(
+            flops=2 * rows * depth * cols, bytes_accessed=6 * depth * cols, transcendentals=0
+        ),
+    )(table, own_table, mix, weights, all_momentum, momentum)
+
+
+def kernel_body(token_ids, table, weights, targets, momentum):
+    owned = momentum.shape[0]
+    mix, all_momentum = mixed_grads(
+        token_ids, table, weights, targets, momentum.astype(jnp.bfloat16)
+    )
+    own_table = lax.dynamic_slice_in_dim(table, lax.axis_index("dp") * owned, owned, 1)
+    return updated(table, own_table, mix, weights, all_momentum, momentum)
+
+
 def solution(mesh):
     placed = (P("dp"), P(), P(None, "tensor"), P("dp", "tensor"), P("dp", "tensor"))
+    small = mesh.shape["dp"] == 8 and mesh.shape["tensor"] == 4
     return jax.shard_map(
-        body,
+        kernel_body if small else body,
         mesh=mesh,
         in_specs=placed,
         out_specs=(P(None, "tensor"), P("dp", "tensor")),

time: 311 us -> 137 us (0.44)
  Pallas kernels: 0 us -> 130 us
  waiting for transfers between devices: 110 us -> 0 us
  matrix products: 63.1 us -> 0 us
  local copies, waits for them, and re-layouts: 58.2 us -> 2.03 us
  blocking collectives: 40.3 us -> 0 us
  between operations: 16.8 us -> 0.64 us
  other arithmetic: 15.1 us -> 3.26 us
  starting transfers between devices: 5.25 us -> 0 us
    pallas_call x0 -> x2, Pallas kernels: none -> 130 us  [the longest x1 107 us: mixed_grads(): pl.pallas_call(mix_kernel, out_shape=(jax.ShapeDtypeStruct((cols, rows),...]
    all_gather x2 -> x0, waiting for transfers between devices: 79.9 us -> none  [the longest x1 71 us: body(): lax.all_gather(momentum.astype(jnp.bfloat16), 'dp', axis=0, tiled=True)]
    dot_general x21 -> x0, matrix products: 63.1 us -> none  [the longest x1 17.2 us: body(): lax.dot_general(table, mixed, (((0,), (0,)), ((), ())), preferred_element...]
    psum x1 -> x0, blocking collectives: 40.3 us -> none  [body(): gram = lax.psum(jnp.stack(gram), ('dp', 'tensor'))]
    unnamed x10 -> x0, local copies, waits for them, and re-layouts: 36.2 us -> none
    all_to_all x1 -> x0, waiting for transfers between devices: 30 us -> none  [body(): own = lax.all_to_all(grads, 'dp', split_axis=1, concat_axis=0, tiled=True)]
    all_gather x1 -> x0, local copies, waits for them, and re-layouts: 17.6 us -> none  [body(): lax.all_gather(momentum.astype(jnp.bfloat16), 'dp', axis=0, tiled=True)]
    reduce_sum x9 -> x0, other arithmetic: 11.7 us -> none  [the longest x1 6.3 us: body(): gram.append(jnp.sum(own.astype(jnp.float32) * mapped[None], axis=(1, 2)))]
  transfers between devices with their start and end apart: 3 -> 0, of which waited for: 3 -> 0; matrix products, arithmetic and copies ran while one was open for 10% -> 0% of each run, Pallas kernels for 0% -> 0%
where the time goes in v2:
time: 137 us; the launch traced here: 136 us
  Pallas kernels  130 us (95%)
  other arithmetic  3.26 us (2%)
  local copies, waits for them, and re-layouts  2.03 us (1%)
    pallas_call x1, Pallas kernels, mixed_grads(): pl.pallas_call(mix_kernel, out_shape=(jax.ShapeDtypeStruct((cols, rows),...  107 us
    pallas_call x1, Pallas kernels, updated(): pl.pallas_call(update_kernel, grid=(depth // tile,), out_shape=(jax.Shape...  23.6 us
    convert_element_type x1, other arithmetic, kernel_body(): momentum.astype(jnp.bfloat16)  3.26 us

profile of v2, /device:TPU:0, one launch (start us, length us, event | category | flops | bytes accessed | tf_op | source)
XLA Modules:
  0.0 136.3 jit_solution(4683851646960744217)
XLA Ops:
  0.6 2.0 %constant_dynamic-slice_fusion.own_table = bf16[512,320]{1,0:T(8,128)(2,1)} fusion(bf16[512,2560]{1,0:T(8,128)(2,1)} %table.3, s32[]{:T(128)S(6)} %select_n.3), kind=kLoop, calls=%fused_computation | loop fusion | bytes 655364 | tf_op jit(solution)/shard_map/dynamic_slice | solution.py:520
  2.7 3.3 %convert_element_type.3.momentum = bf16[320,2560]{1,0:T(8,128)(2,1)} convert(f32[320,2560]{1,0:T(8,128)} %momentum.1) | non-fusion elementwise | flops 819200 | bytes 4915200 | tf_op jit(solution)/shard_map/convert_element_type | solution.py:518
  5.9 106.8 %shard_map.68 = (bf16[2560,512]{1,0:T(8,128)(2,1)}, bf16[2560,2560]{1,0:T(8,128)(2,1)}) custom-call(s32[1,512]{1,0:T(1,128)} %bitcast.1, bf16[512,2560]{1,0:T(8,128)(2,1)} %table.3, bf16[2560,2560]{1,0:T(8,128)(2,1)} %weights.3, bf16[512,2560]{1,0:T(8,128)(2,1)} %targets.1, bf16[320,2560]{1,0:T(8,128)(2,1)} %convert_element_type.3.momentum), custom_call_target="tpu_custom_call" | custom-call | flops 6710886400 | bytes 13107200 | tf_op jit(solution)/shard_map/pallas_call | solution.py:428
  112.7 23.6 %shard_map.69 = (bf16[2560,2560]{1,0:T(8,128)(2,1)}, f32[320,2560]{1,0:T(8,128)}) custom-call(bf16[512,2560]{1,0:T(8,128)(2,1)} %table.3, bf16[512,320]{1,0:T(8,128)(2,1)} %constant_dynamic-slice_fusion.own_table, bf16[2560,512]{1,0:T(8,128)(2,1)} %get-tuple-element.4.mix, bf16[2560,2560]{1,0:T(8,128)(2,1)} %weights.3, ...), custom_call_target="tpu_custom_call" | custom-call | flops 6710886400 | bytes 39321600 | tf_op jit(solution)/shard_map/pallas_call | solution.py:492

commit v3 on v2

--- a/solution.py
+++ b/solution.py
@@ -140,7 +140,7 @@
         ).wait_recv()
 
 
-def exchange(axis, size, value, sent, slots, send, recv):
+def exchange(axis, size, value, sent, slots, send, recv, meanwhile):
     me = lax.axis_index(axis)
     sent[...] = value
     slots[me] = value
@@ -157,6 +157,7 @@
             )
         )
         copies[-1].start()
+    meanwhile()
     for shift in range(1, size):
         origin = lax.rem(me + size - shift, size)
         pltpu.make_async_remote_copy(
@@ -202,10 +203,10 @@
 
 
 def mix_kernel(
-    ids, table, weights, targets, momentum, mix_out, mom_out,
-    wbuf, tbuf, gt, gx, kern_high, kern_low, mapped, sums, coef_buf, mix_own,
+    ids, table, weights, targets, momentum, mix_out, mom_out, turned_out,
+    mom_wide, mom_own, turned, wbuf, tbuf, gt, gx, kern_high, kern_low, mapped, sums, coef_buf, mix_own,
     t_sent, t_slots, d_sent, d_slots,
-    w_sem, t_sem, local_sem, mom_send, mom_recv, mix_send, mix_recv,
+    w_sem, t_sem, m_sem, local_sem, mom_send, mom_recv, mix_send, mix_recv,
     g_send, g_recv, ts_send, ts_recv, ds_send, ds_recv,
 ):
     me = lax.axis_index("dp")
@@ -224,6 +225,18 @@
             pltpu.make_async_copy(targets.at[:, at], tbuf.at[slot], t_sem.at[slot]),
         )
 
+    mom = Gather(me, mom_own, mom_out, mom_send, mom_recv, 4)
+    mix = Gather(me, mix_own, mix_out, mix_send, mix_recv, 2)
+
+    def mom_rows(part):
+        return pl.ds(part * mom.rows, mom.rows)
+
+    def mom_load(part):
+        at = mom_rows(part)
+        return pltpu.make_async_copy(momentum.at[at], mom_wide.at[at], m_sem.at[part])
+
+    for part in (0, 2, 1, 3):
+        mom_load(part).start()
     for load in fetch(0, 0):
         load.start()
 
@@ -236,12 +249,13 @@
         pl.semaphore_signal(
             barrier, inc=1, device_id={"tensor": lax.rem(mine + shift, 4)}, device_id_type=MESH
         )
+    for part in (0, 2, 1, 3):
+        mom_load(part).wait()
+        mom_own[mom_rows(part), :] = mom_wide[mom_rows(part), :].astype(jnp.bfloat16)
     pl.semaphore_wait(barrier, 10)
 
-    mom = Gather(me, momentum, mom_out, mom_send, mom_recv, 4)
-    mix = Gather(me, mix_own, mix_out, mix_send, mix_recv, 2)
     own_rows = pl.ds(pl.multiple_of(me * mom.piece, 16), mom.piece)
-    keep_mom = pltpu.make_async_copy(momentum, mom_out.at[own_rows], local_sem.at[0])
+    keep_mom = pltpu.make_async_copy(mom_own, mom_out.at[own_rows], local_sem.at[0])
     keep_mom.start()
     for part in (0, 1):
         mom.copy(0, part).start()
@@ -298,10 +312,6 @@
     lax.fori_loop(0, 4, grads, 0)
     gx[me] = gt[me]
 
-    for part in (0, 1):
-        mom.copy(1, part).start()
-        mom.copy(0, part + 2).start()
-
     kern = lax.dot_general(
         table[...], table[...], (((1,), (1,)), ((), ())), preferred_element_type=jnp.float32
     )
@@ -309,7 +319,16 @@
     kern_high[...] = high
     kern_low[...] = (kern - high.astype(jnp.float32)).astype(jnp.bfloat16)
 
-    for part in (0, 1):
+    def turn(step, carry):
+        at = pl.ds(pl.multiple_of(step * 256, 256), 256)
+        turned[at, :] = table[:, at].T
+        return carry
+
+    lax.fori_loop(0, table.shape[1] // 256, turn, 0)
+    keep_turned = pltpu.make_async_copy(turned, turned_out, local_sem.at[2])
+    keep_turned.start()
+
+    def relay(part):
         mom.arrived(0, part)
         mom.copy(2, part).start()
         mom.copy(4, part).start()
@@ -347,15 +366,19 @@
         lax.fori_loop(0, bits + 1, pair, 0)
         return carry
 
-    lax.fori_loop(0, 8, grams, 0)
+    lax.fori_loop(0, 7, grams, 0)
+    relay(0)
+    grams(7, 0)
 
     lanes = lax.broadcasted_iota(jnp.int32, (8, 128), 1)
     gram = jnp.zeros((8, 128), jnp.float32)
     for index in range(8):
         column = jnp.sum(sums[index], axis=1, keepdims=True)
         gram = gram + jnp.where(lanes == index, column, 0.0)
-    gram, t_copies = exchange("tensor", 4, gram, t_sent, t_slots, ts_send, ts_recv)
-    gram, d_copies = exchange("dp", 8, gram, d_sent, d_slots, ds_send, ds_recv)
+    gram, t_copies = exchange("tensor", 4, gram, t_sent, t_slots, ts_send, ts_recv, lambda: None)
+    gram, d_copies = exchange(
+        "dp", 8, gram, d_sent, d_slots, ds_send, ds_recv, lambda: relay(1)
+    )
     coef_buf[...] = tree_columns(gram)
 
     for lane in range(gx.shape[2] // 128):
@@ -377,6 +400,9 @@
     mix.copy(1, 0).start()
     for part in (0, 1):
         mix.copy(3, part).start()
+    for part in (0, 1):
+        mom.copy(1, part).start()
+        mom.copy(0, part + 2).start()
 
     mix.arrived(0, 0)
     mix.copy(2, 0).start()
@@ -384,18 +410,18 @@
     mix.arrived(1, 1)
     mix.copy(2, 1).start()
     mix.copy(5, 1).start()
+    mix.arrived(0, 1)
+    mix.copy(4, 1).start()
+    mix.arrived(1, 0)
+    mix.copy(5, 0).start()
+    for part in range(4):
+        mom.arrived(2, part)
+        mom.copy(6, part).start()
     for part in (0, 1):
         mom.arrived(1, part)
         mom.copy(5, part).start()
         mom.arrived(0, part + 2)
         mom.copy(4, part + 2).start()
-    for part in range(4):
-        mom.arrived(2, part)
-        mom.copy(6, part).start()
-    mix.arrived(0, 1)
-    mix.copy(4, 1).start()
-    mix.arrived(1, 0)
-    mix.copy(5, 0).start()
     for part in (0, 1):
         mix.arrived(2, part)
         mix.copy(6, part).start()
@@ -414,6 +440,7 @@
         copy.wait_send()
     keep_mom.wait()
     keep_mix.wait()
+    keep_turned.wait()
 
 
 def mixed_grads(token_ids, table, weights, targets, momentum):
@@ -430,10 +457,14 @@
         out_shape=(
             jax.ShapeDtypeStruct((cols, rows), bf16),
             jax.ShapeDtypeStruct((8 * momentum.shape[0], cols), bf16),
+            jax.ShapeDtypeStruct((depth, rows), bf16),
         ),
         in_specs=[resident, resident, anywhere, anywhere, anywhere],
-        out_specs=(anywhere, anywhere),
+        out_specs=(anywhere, anywhere, anywhere),
         scratch_shapes=[
+            pltpu.VMEM(momentum.shape, f32),
+            pltpu.VMEM(momentum.shape, bf16),
+            pltpu.VMEM((depth, rows), bf16),
             pltpu.VMEM((2, depth, width), bf16),
             pltpu.VMEM((2, targets.shape[0], width), bf16),
             pltpu.VMEM((8, chunk, rows), bf16),
@@ -448,7 +479,7 @@
             pltpu.VMEM((4, 8, 128), f32),
             pltpu.VMEM((8, 128), f32),
             pltpu.VMEM((8, 8, 128), f32),
-            dma((2,)), dma((2,)), dma((2,)),
+            dma((2,)), dma((2,)), dma((4,)), dma((3,)),
             dma((7, 4)), dma((7, 4)), dma((7, 2)), dma((7, 2)),
             dma((8,)), dma((8,)), dma((4,)), dma((4,)), dma((8,)), dma((8,)),
         ],
@@ -461,64 +492,61 @@
     )(token_ids[None, :], table, weights, targets, momentum)
 
 
-def update_kernel(table, own_table, mix, weights, all_momentum, momentum, new_weights, new_momentum):
-    def spread(columns):
-        return lax.dot_general(
-            columns.T, mix[...], (((1,), (1,)), ((), ())), preferred_element_type=jnp.float32
-        )
-
+def update_kernel(
+    turned, mix, weights, all_momentum, momentum, new_weights, new_momentum, mix_turned
+):
     @pl.when(pl.program_id(0) == 0)
     def _():
-        new_momentum[...] = momentum_decay * momentum[...] + spread(own_table[...])
-
-    step = momentum_decay * all_momentum[...].astype(jnp.float32) + spread(table[...])
+        mix_turned[...] = mix[...].T
+
+    adasum = jnp.dot(turned[...], mix_turned[...], preferred_element_type=jnp.float32)
+
+    @pl.when(pl.program_id(0) == lax.axis_index("dp"))
+    def _():
+        new_momentum[...] = momentum_decay * momentum[...] + adasum
+
+    step = momentum_decay * all_momentum[...].astype(jnp.float32) + adasum
     new_weights[...] = (weights[...].astype(jnp.float32) - learning_rate * step).astype(
         jnp.bfloat16
     )
 
 
-def updated(table, own_table, mix, weights, all_momentum, momentum):
-    rows, depth = table.shape
-    cols = weights.shape[1]
-    tile = 256
-    owned = momentum.shape[0]
+def updated(turned, mix, weights, all_momentum, momentum):
+    depth, rows = turned.shape
+    owned, cols = momentum.shape
 
     def whole(shape):
         return pl.BlockSpec(shape, lambda step: (0, 0))
 
-    def by_rows():
-        return pl.BlockSpec((tile, cols), lambda step: (step, 0))
+    def by_rows(width):
+        return pl.BlockSpec((owned, width), lambda step: (step, 0))
 
     return pl.pallas_call(
         update_kernel,
-        grid=(depth // tile,),
+        grid=(depth // owned,),
         out_shape=(
             jax.ShapeDtypeStruct((depth, cols), jnp.bfloat16),
             jax.ShapeDtypeStruct((owned, cols), jnp.float32),
         ),
         in_specs=[
-            pl.BlockSpec((rows, tile), lambda step: (0, step)),
-            whole((rows, owned)),
+            by_rows(rows),
             whole((cols, rows)),
-            by_rows(),
-            by_rows(),
+            by_rows(cols),
+            by_rows(cols),
             whole((owned, cols)),
         ],
-        out_specs=(by_rows(), whole((owned, cols))),
+        out_specs=(by_rows(cols), whole((owned, cols))),
+        scratch_shapes=[pltpu.VMEM((rows, cols), jnp.bfloat16)],
         compiler_params=pltpu.CompilerParams(vmem_limit_bytes=56 * 2**20),
         cost_estimate=pl.CostEstimate(
             flops=2 * rows * depth * cols, bytes_accessed=6 * depth * cols, transcendentals=0
         ),
-    )(table, own_table, mix, weights, all_momentum, momentum)
+    )(turned, mix, weights, all_momentum, momentum)
 
 
 def kernel_body(token_ids, table, weights, targets, momentum):
-    owned = momentum.shape[0]
-    mix, all_momentum = mixed_grads(
-        token_ids, table, weights, targets, momentum.astype(jnp.bfloat16)
-    )
-    own_table = lax.dynamic_slice_in_dim(table, lax.axis_index("dp") * owned, owned, 1)
-    return updated(table, own_table, mix, weights, all_momentum, momentum)
+    mix, all_momentum, turned = mixed_grads(token_ids, table, weights, targets, momentum)
+    return updated(turned, mix, weights, all_momentum, momentum)
 
 
 def solution(mesh):

time: 137 us -> 129 us (0.942)
  other arithmetic: 3.26 us -> 0 us
  local copies, waits for them, and re-layouts: 2.03 us -> 0 us
  Pallas kernels: 130 us -> 128 us
    convert_element_type x1 -> x0, other arithmetic: 3.26 us -> none  [kernel_body(): momentum.astype(jnp.bfloat16)]
    pallas_call x1, Pallas kernels: 107 us -> 104 us  [mixed_grads(): pl.pallas_call(mix_kernel, out_shape=(jax.ShapeDtypeStruct((cols, rows),...]
    dynamic_slice x1 -> x0, local copies, waits for them, and re-layouts: 2.03 us -> none  [kernel_body(): lax.dynamic_slice_in_dim(table, lax.axis_index('dp') * owned, owned, 1)]
where the time goes in v3:
time: 129 us
  Pallas kernels  128 us (99%)
    pallas_call x1, Pallas kernels, mixed_grads(): pl.pallas_call(mix_kernel, out_shape=(jax.ShapeDtypeStruct((cols, rows),...  104 us
    pallas_call x1, Pallas kernels, updated(): pl.pallas_call(update_kernel, grid=(depth // owned,), out_shape=(jax.Shap...  23.9 us

profile of v3, /device:TPU:0, one launch (start us, length us, event | category | flops | bytes accessed | tf_op | source)
XLA Modules:
  0.0 128.8 jit_solution(15127946274476237258)
XLA Ops:
  0.6 104.3 %shard_map.68 = (bf16[2560,512]{1,0:T(8,128)(2,1)}, bf16[2560,2560]{1,0:T(8,128)(2,1)}, bf16[2560,512]{1,0:T(8,128)(2,1)}) custom-call(s32[1,512]{1,0:T(1,128)} %bitcast.1, bf16[512,2560]{1,0:T(8,128)(2,1)} %table.1, bf16[2560,2560]{1,0:T(8,128)(2,1)} %weights.3, bf16[512,2560]{1,0:T(8,128)(2,1)} %targets.1, f32[320,2560]{1,0:T(8,128)} %momentum.3), custom_call_target="tpu_custom_call" | custom-call | flops 6710886400 | bytes 13107200 | tf_op jit(solution)/shard_map/pallas_call | solution.py:455
  104.9 23.9 %shard_map.69 = (bf16[2560,2560]{1,0:T(8,128)(2,1)}, f32[320,2560]{1,0:T(8,128)}) custom-call(bf16[2560,512]{1,0:T(8,128)(2,1)} %get-tuple-element.5.turned, bf16[2560,512]{1,0:T(8,128)(2,1)} %get-tuple-element.6.mix, bf16[2560,2560]{1,0:T(8,128)(2,1)} %weights.3, bf16[2560,2560]{1,0:T(8,128)(2,1)} %get-tuple-element.7.all_momentum, f32[320,2560]{1,0:T(8,128)} %momentum.3), custom_call_target="tpu_custom_call" | custom-call | flops 6710886400 | bytes 39321600 | tf_op jit(solution)/shard_map/pallas_call | solution.py:524

commit v4 on v3

--- a/solution.py
+++ b/solution.py
@@ -96,9 +96,9 @@
 
 
 class Gather:
-    def __init__(self, me, own, out, send, recv, parts):
-        self.me, self.own, self.out, self.send, self.recv = me, own, out, send, recv
-        self.parts, self.piece = parts, own.shape[0]
+    def __init__(self, me, out, send, recv, parts):
+        self.me, self.out, self.send, self.recv = me, out, send, recv
+        self.parts, self.piece = parts, out.shape[0] // 8
         self.rows = self.piece // parts
 
     def place(self, owner, part):
@@ -117,9 +117,8 @@
     def copy(self, kind, part):
         owner, towards = self.moved(kind, part)
         here = self.place(flip(self.me, owner), part)
-        source = self.own.at[pl.ds(part * self.rows, self.rows)] if owner == 0 else here
         return pltpu.make_async_remote_copy(
-            src_ref=source,
+            src_ref=here,
             dst_ref=here,
             send_sem=self.send.at[kind, part],
             recv_sem=self.recv.at[kind, part],
@@ -203,10 +202,11 @@
 
 
 def mix_kernel(
-    ids, table, weights, targets, momentum, mix_out, mom_out, turned_out,
-    mom_wide, mom_own, turned, wbuf, tbuf, gt, gx, kern_high, kern_low, mapped, sums, coef_buf, mix_own,
+    ids, table, weights, targets, momentum, new_weights, new_momentum,
+    mom_wide, mom_all, turned, wbuf, tbuf, gt, gx, kern_high, kern_low, mapped, sums, coef_buf,
+    mix_all, mix_turned, wtile,
     t_sent, t_slots, d_sent, d_slots,
-    w_sem, t_sem, m_sem, local_sem, mom_send, mom_recv, mix_send, mix_recv,
+    w_sem, t_sem, m_sem, local_sem, load_sem, store_sem, mom_send, mom_recv, mix_send, mix_recv,
     g_send, g_recv, ts_send, ts_recv, ds_send, ds_recv,
 ):
     me = lax.axis_index("dp")
@@ -225,8 +225,8 @@
             pltpu.make_async_copy(targets.at[:, at], tbuf.at[slot], t_sem.at[slot]),
         )
 
-    mom = Gather(me, mom_own, mom_out, mom_send, mom_recv, 4)
-    mix = Gather(me, mix_own, mix_out, mix_send, mix_recv, 2)
+    mom = Gather(me, mom_all, mom_send, mom_recv, 4)
+    mix = Gather(me, mix_all, mix_send, mix_recv, 2)
 
     def mom_rows(part):
         return pl.ds(part * mom.rows, mom.rows)
@@ -251,12 +251,10 @@
         )
     for part in (0, 2, 1, 3):
         mom_load(part).wait()
-        mom_own[mom_rows(part), :] = mom_wide[mom_rows(part), :].astype(jnp.bfloat16)
+        mom_place = pl.ds(pl.multiple_of(me * mom.piece + part * mom.rows, 16), mom.rows)
+        mom_all[mom_place, :] = mom_wide[mom_rows(part), :].astype(jnp.bfloat16)
     pl.semaphore_wait(barrier, 10)
 
-    own_rows = pl.ds(pl.multiple_of(me * mom.piece, 16), mom.piece)
-    keep_mom = pltpu.make_async_copy(mom_own, mom_out.at[own_rows], local_sem.at[0])
-    keep_mom.start()
     for part in (0, 1):
         mom.copy(0, part).start()
         mom.copy(1, part + 2).start()
@@ -325,8 +323,60 @@
         return carry
 
     lax.fori_loop(0, table.shape[1] // 256, turn, 0)
-    keep_turned = pltpu.make_async_copy(turned, turned_out, local_sem.at[2])
-    keep_turned.start()
+    half = mom.piece // 2
+    tasks = [(bits, 0, 2 * half) for bits in (0, 6, 1, 7)]
+    tasks += [(2, 0, half), (4, half, half), (3, 0, half), (5, half, half)]
+    tasks += [(2, half, half), (4, 0, half), (3, half, half), (5, 0, half)]
+
+    def task_rows(index):
+        bits, first, count_rows = tasks[index]
+        return pl.ds(pl.multiple_of(flip(me, bits) * mom.piece + first, 16), count_rows)
+
+    def tile(index):
+        return wtile.at[index % 3, pl.ds(0, tasks[index][2])]
+
+    def load(index):
+        return pltpu.make_async_copy(
+            weights.at[task_rows(index)], tile(index), load_sem.at[index % 3]
+        )
+
+    def store(index):
+        return pltpu.make_async_copy(
+            tile(index), new_weights.at[task_rows(index)], store_sem.at[index % 3]
+        )
+
+    keep_mom = pltpu.make_async_copy(mom_wide, new_momentum, local_sem.at[0])
+
+    def update(index):
+        bits, first, count_rows = tasks[index]
+        rows, slot = task_rows(index), index % 3
+        load(index).wait()
+
+        def columns(step, carry):
+            at = pl.ds(pl.multiple_of(step * 512, 512), 512)
+            adasum = jnp.dot(
+                turned[rows, :], mix_turned[:, at], preferred_element_type=jnp.float32
+            )
+            if bits == 0:
+                moved = momentum_decay * mom_wide[:, at] + adasum
+                mom_wide[:, at] = moved
+            else:
+                moved = momentum_decay * mom_all[rows, at].astype(jnp.float32) + adasum
+            old = wtile[slot, 0:count_rows, at].astype(jnp.float32)
+            wtile[slot, 0:count_rows, at] = (old - learning_rate * moved).astype(jnp.bfloat16)
+            return carry
+
+        lax.fori_loop(0, wtile.shape[2] // 512, columns, 0)
+        store(index).start()
+        if bits == 0:
+            keep_mom.start()
+        if index >= 1:
+            store(index - 1).wait()
+            if index + 2 < len(tasks):
+                load(index + 2).start()
+
+    for index in range(3):
+        load(index).start()
 
     def relay(part):
         mom.arrived(0, part)
@@ -381,55 +431,89 @@
     )
     coef_buf[...] = tree_columns(gram)
 
+    own_columns = pl.ds(pl.multiple_of(me * chunk, 16), chunk)
     for lane in range(gx.shape[2] // 128):
         at = pl.ds(lane * 128, 128)
         total = coef_buf[0:1, :] * gx[0, :, at].astype(jnp.float32)
         for index in range(1, 8):
             total = total + coef_buf[index : index + 1, :] * gx[index, :, at].astype(jnp.float32)
-        mix_own[:, at] = total.astype(jnp.bfloat16)
-
-    keep_mix = pltpu.make_async_copy(
-        mix_own,
-        mix_out.at[pl.ds(pl.multiple_of(me * chunk, 16), chunk)],
-        local_sem.at[1],
-    )
-    keep_mix.start()
+        mix_all[own_columns, at] = total.astype(jnp.bfloat16)
+
     mix.copy(0, 0).start()
     mix.copy(1, 1).start()
     mix.copy(0, 1).start()
     mix.copy(1, 0).start()
     for part in (0, 1):
         mix.copy(3, part).start()
-    for part in (0, 1):
-        mom.copy(1, part).start()
-        mom.copy(0, part + 2).start()
-
+    for part in (0, 2):
+        mom.arrived(2, part)
+        mom.copy(6, part).start()
     mix.arrived(0, 0)
     mix.copy(2, 0).start()
     mix.copy(4, 0).start()
     mix.arrived(1, 1)
     mix.copy(2, 1).start()
     mix.copy(5, 1).start()
+    for part in (0, 1):
+        mom.copy(1, part).start()
+        mom.copy(0, part + 2).start()
     mix.arrived(0, 1)
     mix.copy(4, 1).start()
     mix.arrived(1, 0)
     mix.copy(5, 0).start()
-    for part in range(4):
+    for part in (1, 3):
         mom.arrived(2, part)
         mom.copy(6, part).start()
     for part in (0, 1):
+        mix.arrived(2, part)
+        mix.copy(6, part).start()
+    for part in (0, 1):
+        for kind in (3, 4, 5, 6):
+            mix.arrived(kind, part)
+
+    def turn_mix(step, carry):
+        at = pl.ds(pl.multiple_of(step * 256, 256), 256)
+        mix_turned[:, at] = mix_all[at, :].T
+        return carry
+
+    lax.fori_loop(0, mix_all.shape[0] // 256, turn_mix, 0)
+
+    def forward(part):
         mom.arrived(1, part)
         mom.copy(5, part).start()
         mom.arrived(0, part + 2)
         mom.copy(4, part + 2).start()
-    for part in (0, 1):
-        mix.arrived(2, part)
-        mix.copy(6, part).start()
+
+    update(0)
+    update(1)
+    for part in range(4):
+        mom.arrived(3, part)
+    update(2)
+    forward(0)
+    for part in range(4):
+        mom.arrived(6, part)
+    update(3)
+    update(4)
+    update(5)
+    for part in (0, 1):
+        mom.arrived(4, part)
+    update(6)
+    for part in (2, 3):
+        mom.arrived(5, part)
+    update(7)
+    forward(1)
+    update(8)
+    update(9)
+    for part in (2, 3):
+        mom.arrived(4, part)
+    update(10)
+    for part in (0, 1):
+        mom.arrived(5, part)
+    update(11)
+    store(len(tasks) - 1).wait()
 
     for gather in (mom, mix):
         for part in range(gather.parts):
-            for kind in (3, 4, 5, 6):
-                gather.arrived(kind, part)
             for kind in range(7):
                 gather.copy(kind, part).wait_send()
     for step in range(4):
@@ -439,11 +523,9 @@
     for copy in t_copies + d_copies:
         copy.wait_send()
     keep_mom.wait()
-    keep_mix.wait()
-    keep_turned.wait()
-
-
-def mixed_grads(token_ids, table, weights, targets, momentum):
+
+
+def kernel_body(token_ids, table, weights, targets, momentum):
     rows, depth = table.shape
     cols = weights.shape[1]
     chunk = cols // 8
@@ -455,15 +537,14 @@
     return pl.pallas_call(
         mix_kernel,
         out_shape=(
-            jax.ShapeDtypeStruct((cols, rows), bf16),
-            jax.ShapeDtypeStruct((8 * momentum.shape[0], cols), bf16),
-            jax.ShapeDtypeStruct((depth, rows), bf16),
+            jax.ShapeDtypeStruct((depth, cols), bf16),
+            jax.ShapeDtypeStruct(momentum.shape, f32),
         ),
         in_specs=[resident, resident, anywhere, anywhere, anywhere],
-        out_specs=(anywhere, anywhere, anywhere),
+        out_specs=(anywhere, anywhere),
         scratch_shapes=[
             pltpu.VMEM(momentum.shape, f32),
-            pltpu.VMEM(momentum.shape, bf16),
+            pltpu.VMEM((depth, cols), bf16),
             pltpu.VMEM((depth, rows), bf16),
             pltpu.VMEM((2, depth, width), bf16),
             pltpu.VMEM((2, targets.shape[0], width), bf16),
@@ -474,79 +555,24 @@
             pltpu.VMEM((chunk, rows), f32),
             pltpu.VMEM((8, 8, rows), f32),
             pltpu.VMEM((8, 128), f32),
-            pltpu.VMEM((chunk, rows), bf16),
+            pltpu.VMEM((cols, rows), bf16),
+            pltpu.VMEM((rows, cols), bf16),
+            pltpu.VMEM((3, *momentum.shape), bf16),
             pltpu.VMEM((8, 128), f32),
             pltpu.VMEM((4, 8, 128), f32),
             pltpu.VMEM((8, 128), f32),
             pltpu.VMEM((8, 8, 128), f32),
-            dma((2,)), dma((2,)), dma((4,)), dma((3,)),
+            dma((2,)), dma((2,)), dma((4,)), dma((1,)), dma((3,)), dma((3,)),
             dma((7, 4)), dma((7, 4)), dma((7, 2)), dma((7, 2)),
             dma((8,)), dma((8,)), dma((4,)), dma((4,)), dma((8,)), dma((8,)),
         ],
         compiler_params=pltpu.CompilerParams(
-            collective_id=0, has_side_effects=True, vmem_limit_bytes=56 * 2**20
+            collective_id=0, has_side_effects=True, vmem_limit_bytes=60 * 2**20
         ),
         cost_estimate=pl.CostEstimate(
             flops=2 * rows * depth * cols, bytes_accessed=2 * depth * cols, transcendentals=0
         ),
     )(token_ids[None, :], table, weights, targets, momentum)
-
-
-def update_kernel(
-    turned, mix, weights, all_momentum, momentum, new_weights, new_momentum, mix_turned
-):
-    @pl.when(pl.program_id(0) == 0)
-    def _():
-        mix_turned[...] = mix[...].T
-
-    adasum = jnp.dot(turned[...], mix_turned[...], preferred_element_type=jnp.float32)
-
-    @pl.when(pl.program_id(0) == lax.axis_index("dp"))
-    def _():
-        new_momentum[...] = momentum_decay * momentum[...] + adasum
-
-    step = momentum_decay * all_momentum[...].astype(jnp.float32) + adasum
-    new_weights[...] = (weights[...].astype(jnp.float32) - learning_rate * step).astype(
-        jnp.bfloat16
-    )
-
-
-def updated(turned, mix, weights, all_momentum, momentum):
-    depth, rows = turned.shape
-    owned, cols = momentum.shape
-
-    def whole(shape):
-        return pl.BlockSpec(shape, lambda step: (0, 0))
-
-    def by_rows(width):
-        return pl.BlockSpec((owned, width), lambda step: (step, 0))
-
-    return pl.pallas_call(
-        update_kernel,
-        grid=(depth // owned,),
-        out_shape=(
-            jax.ShapeDtypeStruct((depth, cols), jnp.bfloat16),
-            jax.ShapeDtypeStruct((owned, cols), jnp.float32),
-        ),
-        in_specs=[
-            by_rows(rows),
-            whole((cols, rows)),
-            by_rows(cols),
-            by_rows(cols),
-            whole((owned, cols)),
-        ],
-        out_specs=(by_rows(cols), whole((owned, cols))),
-        scratch_shapes=[pltpu.VMEM((rows, cols), jnp.bfloat16)],
-        compiler_params=pltpu.CompilerParams(vmem_limit_bytes=56 * 2**20),
-        cost_estimate=pl.CostEstimate(
-            flops=2 * rows * depth * cols, bytes_accessed=6 * depth * cols, transcendentals=0
-        ),
-    )(turned, mix, weights, all_momentum, momentum)
-
-
-def kernel_body(token_ids, table, weights, targets, momentum):
-    mix, all_momentum, turned = mixed_grads(token_ids, table, weights, targets, momentum)
-    return updated(turned, mix, weights, all_momentum, momentum)
 
 
 def solution(mesh):

time: 129 us -> 123 us (0.953)
  Pallas kernels: 128 us -> 109 us
  local copies, waits for them, and re-layouts: 0 us -> 12.7 us
    pallas_call x2 -> x1, Pallas kernels: 128 us -> 109 us  [kernel_body(): pl.pallas_call(mix_kernel, out_shape=(jax.ShapeDtypeStruct((depth, cols),...]
    unnamed x0 -> x4, local copies, waits for them, and re-layouts: none -> 12.7 us
where the time goes in v4:
time: 123 us; the launch traced here: 122 us
  Pallas kernels  109 us (89%)
  local copies, waits for them, and re-layouts  12.7 us (10%)
    pallas_call x1, Pallas kernels, kernel_body(): pl.pallas_call(mix_kernel, out_shape=(jax.ShapeDtypeStruct((depth, cols),...  109 us
    unnamed x4, local copies, waits for them, and re-layouts  12.7 us

profile of v4, /device:TPU:0, one launch (start us, length us, event | category | flops | bytes accessed | tf_op | source)
XLA Modules:
  0.0 122.5 jit_solution(7734944504269475184)
XLA Ops:
  0.6 109.1 %shard_map.68 = (bf16[2560,2560]{1,0:T(8,128)(2,1)}, f32[320,2560]{1,0:T(8,128)}) custom-call(s32[1,512]{1,0:T(1,128)} %bitcast.1, bf16[512,2560]{1,0:T(8,128)(2,1)} %table.1, bf16[2560,2560]{1,0:T(8,128)(2,1)} %weights.1, bf16[512,2560]{1,0:T(8,128)(2,1)} %targets.1, f32[320,2560]{1,0:T(8,128)} %momentum.1), custom_call_target="tpu_custom_call" | custom-call | flops 6710886400 | bytes 13107200 | tf_op jit(solution)/shard_map/pallas_call | solution.py:537
  109.7 0.0 copy-start
  109.8 11.0 %copy.9 = bf16[2560,2560]{1,0:T(8,128)(2,1)} copy(bf16[2560,2560]{1,0:T(8,128)(2,1)} %get-tuple-element.4) | data formatting | bytes 26214400
  120.8 0.0 copy-done
  120.8 1.7 %copy.10 = f32[320,2560]{1,0:T(8,128)} copy(f32[320,2560]{1,0:T(8,128)S(1)} %copy-done) | data formatting | bytes 6553600
Async XLA Ops:
  109.7 11.0 %copy-start = (f32[320,2560]{1,0:T(8,128)S(1)}, f32[320,2560]{1,0:T(8,128)}, u32[]{:S(2)}) copy-start(f32[320,2560]{1,0:T(8,128)} %get-tuple-element.5) | copy-start | bytes 9830404

commit v5 on v4

--- a/solution.py
+++ b/solution.py
@@ -225,7 +225,7 @@
             pltpu.make_async_copy(targets.at[:, at], tbuf.at[slot], t_sem.at[slot]),
         )
 
-    mom = Gather(me, mom_all, mom_send, mom_recv, 4)
+    mom = Gather(me, mom_all, mom_send, mom_recv, 10)
     mix = Gather(me, mix_all, mix_send, mix_recv, 2)
 
     def mom_rows(part):
@@ -235,7 +235,8 @@
         at = mom_rows(part)
         return pltpu.make_async_copy(momentum.at[at], mom_wide.at[at], m_sem.at[part])
 
-    for part in (0, 2, 1, 3):
+    order = (0, 5, 1, 6, 2, 7, 3, 8, 4, 9)
+    for part in order:
         mom_load(part).start()
     for load in fetch(0, 0):
         load.start()
@@ -249,16 +250,16 @@
         pl.semaphore_signal(
             barrier, inc=1, device_id={"tensor": lax.rem(mine + shift, 4)}, device_id_type=MESH
         )
-    for part in (0, 2, 1, 3):
+    for part in order:
         mom_load(part).wait()
         mom_place = pl.ds(pl.multiple_of(me * mom.piece + part * mom.rows, 16), mom.rows)
         mom_all[mom_place, :] = mom_wide[mom_rows(part), :].astype(jnp.bfloat16)
     pl.semaphore_wait(barrier, 10)
 
-    for part in (0, 1):
+    for part in range(5):
         mom.copy(0, part).start()
-        mom.copy(1, part + 2).start()
-    for part in range(4):
+        mom.copy(1, part + 5).start()
+    for part in range(10):
         mom.copy(3, part).start()
 
     row = lax.broadcasted_iota(jnp.int32, (table.shape[0], ids.shape[1]), 0)
@@ -323,10 +324,13 @@
         return carry
 
     lax.fori_loop(0, table.shape[1] // 256, turn, 0)
-    half = mom.piece // 2
-    tasks = [(bits, 0, 2 * half) for bits in (0, 6, 1, 7)]
+    half, early = 5 * mom.rows, 3 * mom.rows
+    tasks = [(0, 0, 2 * half), (1, 0, 2 * half)]
     tasks += [(2, 0, half), (4, half, half), (3, 0, half), (5, half, half)]
-    tasks += [(2, half, half), (4, 0, half), (3, half, half), (5, 0, half)]
+    tasks += [(6, 0, 2 * half), (7, 0, 2 * half)]
+    for first, size in ((0, early), (early, half - early)):
+        tasks += [(2, half + first, size), (4, first, size)]
+        tasks += [(3, half + first, size), (5, first, size)]
 
     def task_rows(index):
         bits, first, count_rows = tasks[index]
@@ -382,9 +386,9 @@
         mom.arrived(0, part)
         mom.copy(2, part).start()
         mom.copy(4, part).start()
-        mom.arrived(1, part + 2)
-        mom.copy(2, part + 2).start()
-        mom.copy(5, part + 2).start()
+        mom.arrived(1, part + 5)
+        mom.copy(2, part + 5).start()
+        mom.copy(5, part + 5).start()
 
     def grams(bits, carry):
         source = flip(me, bits)
@@ -418,6 +422,7 @@
 
     lax.fori_loop(0, 7, grams, 0)
     relay(0)
+    relay(1)
     grams(7, 0)
 
     lanes = lax.broadcasted_iota(jnp.int32, (8, 128), 1)
@@ -427,7 +432,7 @@
         gram = gram + jnp.where(lanes == index, column, 0.0)
     gram, t_copies = exchange("tensor", 4, gram, t_sent, t_slots, ts_send, ts_recv, lambda: None)
     gram, d_copies = exchange(
-        "dp", 8, gram, d_sent, d_slots, ds_send, ds_recv, lambda: relay(1)
+        "dp", 8, gram, d_sent, d_slots, ds_send, ds_recv, lambda: relay(2)
     )
     coef_buf[...] = tree_columns(gram)
 
@@ -445,7 +450,8 @@
     mix.copy(1, 0).start()
     for part in (0, 1):
         mix.copy(3, part).start()
-    for part in (0, 2):
+    relay(3)
+    for part in (0, 1, 5, 6):
         mom.arrived(2, part)
         mom.copy(6, part).start()
     mix.arrived(0, 0)
@@ -454,14 +460,15 @@
     mix.arrived(1, 1)
     mix.copy(2, 1).start()
     mix.copy(5, 1).start()
-    for part in (0, 1):
+    relay(4)
+    for part in range(5):
         mom.copy(1, part).start()
-        mom.copy(0, part + 2).start()
+        mom.copy(0, part + 5).start()
     mix.arrived(0, 1)
     mix.copy(4, 1).start()
     mix.arrived(1, 0)
     mix.copy(5, 0).start()
-    for part in (1, 3):
+    for part in (2, 3, 7, 8):
         mom.arrived(2, part)
         mom.copy(6, part).start()
     for part in (0, 1):
@@ -481,35 +488,45 @@
     def forward(part):
         mom.arrived(1, part)
         mom.copy(5, part).start()
-        mom.arrived(0, part + 2)
-        mom.copy(4, part + 2).start()
+        mom.arrived(0, part + 5)
+        mom.copy(4, part + 5).start()
+
+    def landed(kind, parts):
+        for part in parts:
+            mom.arrived(kind, part)
 
     update(0)
+    landed(3, range(10))
     update(1)
-    for part in range(4):
-        mom.arrived(3, part)
+    forward(0)
     update(2)
-    forward(0)
-    for part in range(4):
-        mom.arrived(6, part)
     update(3)
+    forward(1)
+    landed(4, range(5))
     update(4)
+    landed(5, range(5, 10))
     update(5)
-    for part in (0, 1):
-        mom.arrived(4, part)
+    for part in (4, 9):
+        mom.arrived(2, part)
+        mom.copy(6, part).start()
     update(6)
-    for part in (2, 3):
-        mom.arrived(5, part)
+    forward(2)
+    landed(6, range(10))
     update(7)
-    forward(1)
     update(8)
     update(9)
-    for part in (2, 3):
-        mom.arrived(4, part)
+    forward(3)
+    landed(4, range(5, 8))
     update(10)
-    for part in (0, 1):
-        mom.arrived(5, part)
+    landed(5, range(3))
     update(11)
+    forward(4)
+    update(12)
+    update(13)
+    landed(4, range(8, 10))
+    update(14)
+    landed(5, range(3, 5))
+    update(15)
     store(len(tasks) - 1).wait()
 
     for gather in (mom, mix):
@@ -562,8 +579,8 @@
             pltpu.VMEM((4, 8, 128), f32),
             pltpu.VMEM((8, 128), f32),
             pltpu.VMEM((8, 8, 128), f32),
-            dma((2,)), dma((2,)), dma((4,)), dma((1,)), dma((3,)), dma((3,)),
-            dma((7, 4)), dma((7, 4)), dma((7, 2)), dma((7, 2)),
+            dma((2,)), dma((2,)), dma((10,)), dma((1,)), dma((3,)), dma((3,)),
+            dma((7, 10)), dma((7, 10)), dma((7, 2)), dma((7, 2)),
             dma((8,)), dma((8,)), dma((4,)), dma((4,)), dma((8,)), dma((8,)),
         ],
         compiler_params=pltpu.CompilerParams(

time: 123 us -> 124 us (level)
  no operation moved by 1% of the time
where the time goes in v5:
time: 124 us; the launch traced here: 123 us
  Pallas kernels  110 us (89%)
  local copies, waits for them, and re-layouts  12.7 us (10%)
    pallas_call x1, Pallas kernels, kernel_body(): pl.pallas_call(mix_kernel, out_shape=(jax.ShapeDtypeStruct((depth, cols),...  110 us
    unnamed x4, local copies, waits for them, and re-layouts  12.7 us

profile of v5, /device:TPU:0, one launch (start us, length us, event | category | flops | bytes accessed | tf_op | source)
XLA Modules:
  0.0 123.5 jit_solution(8068395782466815246)
XLA Ops:
  0.6 110.1 %shard_map.68 = (bf16[2560,2560]{1,0:T(8,128)(2,1)}, f32[320,2560]{1,0:T(8,128)}) custom-call(s32[1,512]{1,0:T(1,128)} %bitcast.1, bf16[512,2560]{1,0:T(8,128)(2,1)} %table.1, bf16[2560,2560]{1,0:T(8,128)(2,1)} %weights.1, bf16[512,2560]{1,0:T(8,128)(2,1)} %targets.1, f32[320,2560]{1,0:T(8,128)} %momentum.1), custom_call_target="tpu_custom_call" | custom-call | flops 6710886400 | bytes 13107200 | tf_op jit(solution)/shard_map/pallas_call | solution.py:554
  110.7 0.0 copy-start
  110.7 11.0 %copy.9 = bf16[2560,2560]{1,0:T(8,128)(2,1)} copy(bf16[2560,2560]{1,0:T(8,128)(2,1)} %get-tuple-element.4) | data formatting | bytes 26214400
  121.7 0.0 copy-done
  121.7 1.7 %copy.10 = f32[320,2560]{1,0:T(8,128)} copy(f32[320,2560]{1,0:T(8,128)S(1)} %copy-done) | data formatting | bytes 6553600
Async XLA Ops:
  110.7 11.0 %copy-start = (f32[320,2560]{1,0:T(8,128)S(1)}, f32[320,2560]{1,0:T(8,128)}, u32[]{:S(2)}) copy-start(f32[320,2560]{1,0:T(8,128)} %get-tuple-element.5) | copy-start | bytes 9830404
